TPU v7x, 32 devices: a whole 2x2x4 slice. The times are simulated.
32 devices in a mesh: ty: 4 (over x, core), tx: 8 (over z, y).
Axes of the slice: x: 2, y: 2, z: 4, core: 2. Of those that a mesh axis runs over, the one named last changes fastest.
Arguments:
- gaussians: float32 [3072, 59, 128], P(('ty', 'tx')), may hold values from -14 to 18, as said below
- tile_lists: int32 [4, 8, 24], P('ty', 'tx'), may hold values from 0 to 3071, as said below
- tile_counts: int32 [4, 8], P('ty', 'tx'), may hold values from 3 to 24, as said below
- depth_order: int32 [3072], replicated, may hold values from 0 to 3071, as said below
- target: float32 [3, 128, 256], P(None, 'ty', 'tx'), may hold values from 0 to 1
Outputs:
- gaussian_grads: float32 [3072, 59, 128], P(('ty', 'tx'))
- loss: float32 [], replicated
Inputs may be any that keep to these rules, and one draw needn't show every extreme that they name: `tile_lists`: entries beyond a tile's count are arbitrary ranks. The live entries of a tile are rising depth ranks of blocks owned by devices in the tile's own row of ty (block b belongs to device b // 96 of ty+tx, ty slowest). At most 3 live entries of one tile name blocks of one owner; in every row some owner is named 3 times by every tile of the row. No block is live in two entries. `tile_counts`: some tile has 24 in every draw. A permutation: depth_order[r] is the block at depth rank r. `gaussians`: row 2 (Z) lies between 1.5 and 12, row 6 (the quaternion's w) between 0.5 and 1.5.
All inputs are finite; a program needn't handle non-finite values.
Results may differ from a plain program's by a relative error of at most 0.0003.
Values sent between devices are 32-bit elements; how exact they have to be, the bound alone decides.
No kernel may reach another device: no remote copies, remote signals or barrier semaphores. Data moves between devices by JAX's collectives and lax.ppermute only.
A program may use at most 64 MiB of HBM per device.

v0:
```python
import jax
import jax.numpy as jnp
from jax import lax
from jax.sharding import PartitionSpec as P

GROUP = 4
CAP = 3


FOCAL = 1000.0
LOW_PASS = 0.3
STRUCT_WEIGHT = 0.2
LUMA_TERM = 0.0001
CONTRAST_TERM = 0.0009
ROBUST_TERM = 1e-06
HARMONIC_ZERO = 0.28209479177387814
HARMONIC_ONE = 0.4886025119029199
HARMONIC_TWO = (
    1.0925484305920792,
    -1.0925484305920792,
    0.31539156525252005,
    -1.0925484305920792,
    0.5462742152960396,
)
HARMONIC_THREE = (
    -0.5900435899266435,
    2.890611442640554,
    -0.4570457994644658,
    0.3731763325901154,
    -0.4570457994644658,
    1.445305721320277,
    -0.5900435899266435,
)


def extended(x, sides, width):
    for axis, dim in sides:
        size, length = (lax.axis_size(axis), x.shape[dim])
        up = [(i, (i + 1) % size) for i in range(size - 1)]
        down = [(j, i) for i, j in up]
        last = lax.slice_in_dim(x, length - width, length, axis=dim)
        first = lax.slice_in_dim(x, 0, width, axis=dim)
        before = lax.ppermute(last, axis, up)
        after = lax.ppermute(first, axis, down)
        x = jnp.concatenate([before, x, after], axis=dim)
    return x


def harmonics(dir_x, dir_y, dir_z):
    square_x = dir_x * dir_x
    square_y = dir_y * dir_y
    square_z = dir_z * dir_z
    pair_xy = dir_x * dir_y
    pair_yz = dir_y * dir_z
    pair_xz = dir_x * dir_z
    return jnp.stack(
        [
            HARMONIC_ZERO * jnp.ones_like(dir_x),
            -HARMONIC_ONE * dir_y,
            HARMONIC_ONE * dir_z,
            -HARMONIC_ONE * dir_x,
            HARMONIC_TWO[0] * pair_xy,
            HARMONIC_TWO[1] * pair_yz,
            HARMONIC_TWO[2] * (2.0 * square_z - square_x - square_y),
            HARMONIC_TWO[3] * pair_xz,
            HARMONIC_TWO[4] * (square_x - square_y),
            HARMONIC_THREE[0] * dir_y * (3.0 * square_x - square_y),
            HARMONIC_THREE[1] * pair_xy * dir_z,
            HARMONIC_THREE[2] * dir_y * (4.0 * square_z - square_x - square_y),
            HARMONIC_THREE[3] * dir_z * (2.0 * square_z - 3.0 * square_x - 3.0 * square_y),
            HARMONIC_THREE[4] * dir_x * (4.0 * square_z - square_x - square_y),
            HARMONIC_THREE[5] * dir_z * (square_x - square_y),
            HARMONIC_THREE[6] * dir_x * (square_x - 3.0 * square_y),
        ],
        axis=1,
    )


def project(raw, center_x, center_y):
    count_rows = raw.shape[0]
    block = raw.shape[2]
    mean_x, mean_y, mean_z = (raw[:, 0], raw[:, 1], raw[:, 2])
    scale = jnp.exp(raw[:, 3:6])
    quat = raw[:, 6:10] / jnp.sqrt(jnp.sum(raw[:, 6:10] * raw[:, 6:10], axis=1, keepdims=True))
    real, imag_i, imag_j, imag_k = (quat[:, 0], quat[:, 1], quat[:, 2], quat[:, 3])
    rotation = [
        [
            1.0 - 2.0 * (imag_j * imag_j + imag_k * imag_k),
            2.0 * (imag_i * imag_j - real * imag_k),
            2.0 * (imag_i * imag_k + real * imag_j),
        ],
        [
            2.0 * (imag_i * imag_j + real * imag_k),
            1.0 - 2.0 * (imag_i * imag_i + imag_k * imag_k),
            2.0 * (imag_j * imag_k - real * imag_i),
        ],
        [
            2.0 * (imag_i * imag_k - real * imag_j),
            2.0 * (imag_j * imag_k + real * imag_i),
            1.0 - 2.0 * (imag_i * imag_i + imag_j * imag_j),
        ],
    ]
    scaled = [[rotation[row][col] * scale[:, col] for col in range(3)] for row in range(3)]
    sigma = [
        [sum((scaled[row][col] * scaled[other][col] for col in range(3))) for other in range(3)]
        for row in range(3)
    ]
    inverse_z = 1.0 / mean_z
    jac_diag = FOCAL * inverse_z
    jac_xz = -FOCAL * mean_x * inverse_z * inverse_z
    jac_yz = -FOCAL * mean_y * inverse_z * inverse_z
    row_u = [jac_diag * sigma[0][col] + jac_xz * sigma[2][col] for col in range(3)]
    row_v = [jac_diag * sigma[1][col] + jac_yz * sigma[2][col] for col in range(3)]
    cov_uu = row_u[0] * jac_diag + row_u[2] * jac_xz + LOW_PASS
    cov_uv = row_u[1] * jac_diag + row_u[2] * jac_yz
    cov_vv = row_v[1] * jac_diag + row_v[2] * jac_yz + LOW_PASS
    determinant = cov_uu * cov_vv - cov_uv * cov_uv
    pos_u = FOCAL * mean_x * inverse_z + center_x
    pos_v = FOCAL * mean_y * inverse_z + center_y
    opacity = 0.99 * jax.nn.sigmoid(raw[:, 10])
    length = jnp.sqrt(mean_x * mean_x + mean_y * mean_y + mean_z * mean_z)
    basis = harmonics(mean_x / length, mean_y / length, mean_z / length)
    coeffs = raw[:, 11:59].reshape(count_rows, 16, 3, block)
    color = 0.5 + jnp.sum(coeffs * basis[:, :, None, :], axis=1)
    shape_rows = jnp.stack(
        [pos_u, pos_v, cov_vv / determinant, -cov_uv / determinant, cov_uu / determinant, opacity],
        axis=1,
    )
    return jnp.concatenate([shape_rows, color], axis=1)


def composite(flat, live, pixel_x, pixel_y):
    delta_x = pixel_x[None, :] - flat[0][:, None]
    delta_y = pixel_y[None, :] - flat[1][:, None]
    power = (
        flat[2][:, None] * delta_x * delta_x
        + 2.0 * flat[3][:, None] * delta_x * delta_y
        + flat[4][:, None] * delta_y * delta_y
    )
    alpha = (live * flat[5])[:, None] * jnp.exp(-0.5 * power)
    keep = jnp.log1p(-alpha)
    before = jnp.cumsum(keep, axis=0) - keep
    weight = alpha * jnp.exp(before)
    color = jnp.dot(
        flat[6:9], weight, precision=lax.Precision.HIGHEST, preferred_element_type=jnp.float32
    )
    return (color, jnp.sum(keep, axis=0))


def to_groups(slot_flat, live):
    lmax, fields, block = slot_flat.shape
    steps_total = lmax // GROUP
    groups = (
        slot_flat.reshape(steps_total, GROUP, fields, block)
        .transpose(0, 2, 1, 3)
        .reshape(steps_total, fields, GROUP * block)
    )
    live_groups = jnp.repeat(live.astype(jnp.float32), block).reshape(steps_total, GROUP * block)
    return (groups, live_groups)


def from_groups(grads, block):
    steps_total, fields, spread = grads.shape
    return (
        grads.reshape(steps_total, fields, GROUP, block)
        .transpose(0, 2, 1, 3)
        .reshape(steps_total * GROUP, fields, block)
    )


def render_forward(groups, live_groups, used, pixel_x, pixel_y):
    pixels = pixel_x.shape[0]

    def advance(index, carry):
        color, log_light, store = carry
        group_color, log_keep = composite(groups[index], live_groups[index], pixel_x, pixel_y)
        store = store.at[index].set(log_light)
        return (color + jnp.exp(log_light)[None, :] * group_color, log_light + log_keep, store)

    start = (
        jnp.zeros((3, pixels), jnp.float32),
        jnp.zeros((pixels,), jnp.float32),
        jnp.zeros((groups.shape[0], pixels), jnp.float32),
    )
    color, final_light, store = lax.fori_loop(0, used, advance, start)
    return (color, store)


def render_backward(groups, live_groups, used, store, pixel_x, pixel_y, color_grad):

    def retreat(step, carry):
        behind, grads = carry
        index = used - 1 - step
        live_now = live_groups[index]

        def shade(flat):
            return composite(flat, live_now, pixel_x, pixel_y)

        (group_color, log_keep), pull = jax.vjp(shade, groups[index])
        light = jnp.exp(store[index])
        passed = light * jnp.exp(log_keep)
        flat_grad = pull(
            (light[None, :] * color_grad, passed * jnp.sum(color_grad * behind, axis=0))
        )[0]
        behind = group_color + jnp.exp(log_keep)[None, :] * behind
        return (behind, grads.at[index].set(flat_grad))

    start = (jnp.zeros_like(color_grad), jnp.zeros_like(groups))
    return lax.fori_loop(0, used, retreat, start)[1]


def window_taps():
    offsets = jnp.arange(11, dtype=jnp.float32) - 5.0
    taps = jnp.exp(-offsets * offsets / 4.5)
    return taps / jnp.sum(taps)


def filtered(field, taps):
    rows = field.shape[-2] - 10
    cols = field.shape[-1] - 10
    sideways = sum((taps[shift] * field[..., :, shift : shift + cols] for shift in range(11)))
    return sum((taps[shift] * sideways[..., shift : shift + rows, :] for shift in range(11)))


def similarity(mean_a, mean_b, square_a, square_b, cross):
    var_a = square_a - mean_a * mean_a
    var_b = square_b - mean_b * mean_b
    covar = cross - mean_a * mean_b
    top = (2.0 * mean_a * mean_b + LUMA_TERM) * (2.0 * covar + CONTRAST_TERM)
    bottom = (mean_a * mean_a + mean_b * mean_b + LUMA_TERM) * (var_a + var_b + CONTRAST_TERM)
    return top / bottom


def moments(picture, goal, taps):
    return (
        filtered(picture, taps),
        filtered(goal, taps),
        filtered(picture * picture, taps),
        filtered(goal * goal, taps),
        filtered(picture * goal, taps),
    )


def per_device(gaussians, tile_lists, tile_counts, depth_order, target):
    owned = gaussians.shape[0]
    fields = gaussians.shape[1]
    block = gaussians.shape[2]
    lmax = tile_lists.shape[2]
    side = target.shape[1]
    across = lax.axis_size("tx")
    row_index = lax.axis_index("ty")
    col_index = lax.axis_index("tx")
    height = side * lax.axis_size("ty")
    width = side * across
    center_x = 0.5 * width
    center_y = 0.5 * height
    capacity = CAP

    def projector(raw):
        return project(raw, center_x, center_y)

    ranks = tile_lists.reshape(lmax)
    count = tile_counts.reshape(())
    live = jnp.arange(lmax, dtype=jnp.int32) < count
    blocks = depth_order[ranks]
    owner = blocks // owned - row_index * across
    local = blocks % owned
    hits = (
        (owner[:, None] == jnp.arange(across, dtype=jnp.int32)[None, :]) & live[:, None]
    ).astype(jnp.int32)
    position = jnp.sum((jnp.cumsum(hits, axis=0) - hits) * hits, axis=1)
    slot_index = jnp.where(live, owner * capacity + position, across * capacity)
    request = jnp.full((across * capacity,), -1, jnp.int32).at[slot_index].set(local, mode="drop")
    asked = lax.all_to_all(
        request.reshape(across, capacity), "tx", split_axis=0, concat_axis=0, tiled=True
    ).reshape(across * capacity)
    valid = asked >= 0
    served = gaussians[jnp.maximum(asked, 0)]
    pick = jnp.where(live, slot_index, 0)
    fetched = lax.all_to_all(
        served.reshape(across, capacity, fields, block),
        "tx",
        split_axis=0,
        concat_axis=0,
        tiled=True,
    ).reshape(across * capacity, fields, block)
    slot_flat, pull_raw = jax.vjp(projector, fetched[pick])
    offsets = jnp.arange(side * side, dtype=jnp.int32)
    pixel_x = (col_index * side + offsets % side).astype(jnp.float32) + 0.5
    pixel_y = (row_index * side + offsets // side).astype(jnp.float32) + 0.5
    groups, live_groups = to_groups(slot_flat, live)
    used = (count + GROUP - 1) // GROUP
    color, store = render_forward(groups, live_groups, used, pixel_x, pixel_y)
    image = color.reshape(3, side, side)
    taps = window_taps()
    stacked = jnp.stack([image, target])
    framed = extended(stacked, (("ty", 2), ("tx", 3)), 10)
    maps = moments(framed[0], framed[1], taps)
    score, pull_score = jax.vjp(similarity, *maps)
    parts = pull_score(jnp.full_like(score, -STRUCT_WEIGHT))
    rows_at = row_index * side - 5 + jnp.arange(side + 10, dtype=jnp.int32)
    cols_at = col_index * side - 5 + jnp.arange(side + 10, dtype=jnp.int32)
    inside = ((rows_at >= 0) & (rows_at < height))[:, None] & ((cols_at >= 0) & (cols_at < width))[
        None, :
    ]
    coeffs = jnp.stack([parts[0], parts[2], parts[4]]) * inside.astype(jnp.float32)
    smoothed = filtered(coeffs, taps)
    score = score[:, 5:-5, 5:-5]
    gap = image - target
    robust = jnp.sqrt(gap * gap + ROBUST_TERM)
    local_total = jnp.sum((1.0 - STRUCT_WEIGHT) * robust + STRUCT_WEIGHT * (1.0 - score))
    image_grad = (
        smoothed[0]
        + 2.0 * image * smoothed[1]
        + target * smoothed[2]
        + (1.0 - STRUCT_WEIGHT) * gap / robust
    )
    total = lax.psum(local_total, ("ty", "tx"))
    flat_grads = render_backward(
        groups, live_groups, used, store, pixel_x, pixel_y, image_grad.reshape(3, side * side)
    )
    slot_grads = from_groups(flat_grads, block)
    raw_slot = pull_raw(slot_grads)[0]
    reply = (
        jnp.zeros((across * capacity, fields, block), jnp.float32)
        .at[slot_index]
        .set(raw_slot, mode="drop")
    )
    raw_grads = lax.all_to_all(
        reply.reshape(across, capacity, fields, block),
        "tx",
        split_axis=0,
        concat_axis=0,
        tiled=True,
    ).reshape(across * capacity, fields, block)
    destination = jnp.where(valid, asked, owned)
    gaussian_grads = jnp.zeros_like(gaussians).at[destination].add(raw_grads, mode="drop")
    return (gaussian_grads, total / (3.0 * height * width))


def solution(mesh):
    return jax.shard_map(
        per_device,
        mesh=mesh,
        in_specs=(
            P(("ty", "tx"), None, None),
            P("ty", "tx", None),
            P("ty", "tx"),
            P(),
            P(None, "ty", "tx"),
        ),
        out_specs=(P(("ty", "tx"), None, None), P()),
        check_vma=False,
    )
```

profile of v0, /device:TPU:0, one launch (start us, length us, event | category | flops | bytes accessed | tf_op | source)
XLA Modules:
  0.0 652.0 jit_solution(4778044072565028751)
XLA Ops:
  4.7 13.5 %all_to_all.19 = s32[8,1,3]{2,1,0:T(1,128)S(1)} all-to-all(s32[8,1,3]{2,1,0:T(1,128)S(1)} %bitcast.468), channel_id=1, replica_groups=mesh['ty'=4,'tx'=8] {'tx'}, dimensions={0} | all-to-all | bytes 192 | tf_op jit(solution)/shard_map/all_to_all | solution.py:274
  31.3 17.7 %all-to-all-done.1 = f32[8,3,59,128]{3,2,1,0:T(8,128)} async-done(((f32[8,3,59,128]{3,2,1,0:T(8,128)}), f32[8,3,59,128]{3,2,1,0:T(8,128)}, u32[]{:S(2)}, u32[]{:S(2)}) %all-to-all-start.1) | async-done | bytes 725024 | tf_op jit(solution)/shard_map/all_to_all | solution.py:280
  60.2 87.7 %while.32 = (s32[]{:T(128)}, f32[3,1024]{1,0:T(4,128)S(1)}, f32[1024]{0:T(1024)S(1)}, f32[6,1024]{1,0:T(8,128)S(1)}, s32[]{:T(128)}, /*index=5*/f32[6,9,512]{2,1...) while((s32[]{:T(128)}, f32[3,1024]{1,0:T(4,128)S(1)}, ...), condition=%wide.region_10.11_spmd.clone, body=%wide.region_5.10_spmd.clone.sunk | while | flops 101230096 | bytes 25543560 | solution.py:185
  148.5 17.0 %collective-permute-start = (f32[2,3,10,32]{3,2,1,0:T(8,128)S(1)}, f32[2,3,10,32]{3,2,1,0:T(8,128)S(1)}, u32[]{:S(2)}, u32[]{:S(2)}) collective-permute-start(f32[2,3,10,32]{3,2,1,0:T(8,128)S(1)} %get-tuple-element.487), channel_id=1, source_target_pairs={{0,8},{8,16},{16,24},{1,9},{9,17},{17,25},{2,10},{10,18},{18,26},{... | collective-permute-start | bytes 23048 | tf_op jit(solution)/shard_map/ppermute | solution.py:43
  184.0 7.2 %fusion.144 = f32[3,52,42]{2,1,0:T(8,128)S(1)} fusion(f32[3,52,52]{2,1,0:T(8,128)S(1)} %get-tuple-element.476, f32[]{:T(128)} %bitcast.34, f32[]{:T(128)} %bitcast.33, f32[]{:T(128)} %bitcast.32, f32[]{:T(128)} %bitcast.31, f32[]{:T(128)} %bitcast.30, f32[]{:T(128)} %bitcast.29, f32[]{:T(128)} %bitcast.28, f32[]{:T(128)} %bitcast.27, f32[]{:T(128)} %bitcast.26, ...), kind=kLoop, calls=%fused_computation.264 | loop fusion | flops 137592 | bytes 314540 | tf_op jit(solution)/shard_map/add | solution.py:221
  191.2 7.2 %fusion.174 = f32[3,52,42]{2,1,0:T(8,128)S(1)} fusion(f32[3,52,52]{2,1,0:T(8,128)S(1)} %get-tuple-element.477, f32[]{:T(128)} %bitcast.34, f32[]{:T(128)} %bitcast.33, f32[]{:T(128)} %bitcast.32, f32[]{:T(128)} %bitcast.31, f32[]{:T(128)} %bitcast.30, f32[]{:T(128)} %bitcast.29, f32[]{:T(128)} %bitcast.28, f32[]{:T(128)} %bitcast.27, f32[]{:T(128)} %bitcast.26, ...), kind=kLoop, calls=%fused_computation.327 | loop fusion | flops 137592 | bytes 314540 | tf_op jit(solution)/shard_map/add | solution.py:221
  198.4 7.2 %fusion.184 = f32[3,52,42]{2,1,0:T(8,128)S(1)} fusion(f32[3,52,52]{2,1,0:T(8,128)S(1)} %get-tuple-element.478, f32[]{:T(128)} %bitcast.34, f32[]{:T(128)} %bitcast.33, f32[]{:T(128)} %bitcast.32, f32[]{:T(128)} %bitcast.31, f32[]{:T(128)} %bitcast.30, f32[]{:T(128)} %bitcast.29, f32[]{:T(128)} %bitcast.28, f32[]{:T(128)} %bitcast.27, f32[]{:T(128)} %bitcast.26, ...), kind=kLoop, calls=%fused_computation.349 | loop fusion | flops 137592 | bytes 314540 | tf_op jit(solution)/shard_map/add | solution.py:221
  205.7 7.2 %fusion.154 = f32[3,52,42]{2,1,0:T(8,128)S(1)} fusion(f32[3,52,52]{2,1,0:T(8,128)S(1)} %get-tuple-element.475, f32[]{:T(128)} %bitcast.34, f32[]{:T(128)} %bitcast.33, f32[]{:T(128)} %bitcast.32, f32[]{:T(128)} %bitcast.31, f32[]{:T(128)} %bitcast.30, f32[]{:T(128)} %bitcast.29, f32[]{:T(128)} %bitcast.28, f32[]{:T(128)} %bitcast.27, f32[]{:T(128)} %bitcast.26, ...), kind=kLoop, calls=%fused_computation.285 | loop fusion | flops 137592 | bytes 314540 | tf_op jit(solution)/shard_map/add | solution.py:221
  212.9 7.2 %fusion.164 = f32[3,52,42]{2,1,0:T(8,128)S(1)} fusion(f32[3,52,52]{2,1,0:T(8,128)S(1)} %get-tuple-element.474, f32[]{:T(128)} %bitcast.34, f32[]{:T(128)} %bitcast.33, f32[]{:T(128)} %bitcast.32, f32[]{:T(128)} %bitcast.31, f32[]{:T(128)} %bitcast.30, f32[]{:T(128)} %bitcast.29, f32[]{:T(128)} %bitcast.28, f32[]{:T(128)} %bitcast.27, f32[]{:T(128)} %bitcast.26, ...), kind=kLoop, calls=%fused_computation.306 | loop fusion | flops 137592 | bytes 314540 | tf_op jit(solution)/shard_map/add | solution.py:221
  220.1 7.2 %fusion.265 = (f32[3,42,42]{2,1,0:T(8,128)S(1)}, f32[3,42,42]{2,1,0:T(8,128)S(1)}, f32[3,42,42]{2,1,0:T(8,128)S(1)}, f32[3,42,42]{2,1,0:T(8,128)S(1)}) fusion(f32[3,52,42]{2,1,0:T(8,128)S(1)} %fusion.144, f32[]{:T(128)} %bitcast.34, f32[]{:T(128)} %bitcast.33, f32[]{:T(128)} %bitcast.32, f32[]{:T(128)} %bitcast.31, f32[]{:T(128)} %bitcast.30, f32[]{:T(128)} %bitcast.29, ...), kind=kLoop, calls=%fused_computation.537 | loop fusion | flops 375732 | bytes 783260 | tf_op jit(solution)/shard_map/jvp()/mul | solution.py:229
  227.4 7.1 %fusion.267 = (f32[3,42,42]{2,1,0:T(8,128)S(1)}, f32[3,42,42]{2,1,0:T(8,128)S(1)}) fusion(f32[3,42,42]{2,1,0:T(8,128)S(1)} %get-tuple-element.371, f32[3,42,42]{2,1,0:T(8,128)S(1)} %get-tuple-element.370, f32[3,52,42]{2,1,0:T(8,128)S(1)} %fusion.154, f32[3,52,42]{2,1,0:T(8,128)S(1)} %fusion.164, f32[]{:T(128)} %bitcast.34, f32[]{:T(128)} %bitcast.33, ...), kind=kLoop, calls=%fused_computation.540 | loop fusion | flops 269892 | bytes 550412 | tf_op jit(solution)/shard_map/jvp()/mul | solution.py:230
  234.7 7.6 %fusion.124 = f32[3,3,42,32]{3,2,1,0:T(8,128)S(1)} fusion(f32[3,3,42,42]{3,2,1,0:T(8,128)S(1)} %maximum_multiply_fusion, f32[]{:T(128)} %bitcast.34, f32[]{:T(128)} %bitcast.33, f32[]{:T(128)} %bitcast.32, f32[]{:T(128)} %bitcast.31, f32[]{:T(128)} %bitcast.30, f32[]{:T(128)} %bitcast.29, f32[]{:T(128)} %bitcast.28, f32[]{:T(128)} %bitcast.27, f32[]{:T(128)} %bitcast.26, ...), kind=kLoop, calls=%fused_computation.215 | loop fusion | flops 254016 | bytes 580652 | tf_op jit(solution)/shard_map/add | solution.py:221
  242.3 7.1 %fusion.134 = f32[3,3,32,32]{3,2,1,0:T(8,128)S(1)} fusion(f32[3,3,42,32]{3,2,1,0:T(8,128)S(1)} %fusion.124, f32[]{:T(128)} %bitcast.34, f32[]{:T(128)} %bitcast.33, f32[]{:T(128)} %bitcast.32, f32[]{:T(128)} %bitcast.31, f32[]{:T(128)} %bitcast.30, f32[]{:T(128)} %bitcast.29, f32[]{:T(128)} %bitcast.28, f32[]{:T(128)} %bitcast.27, f32[]{:T(128)} %bitcast.26, ...), kind=kLoop, calls=%fused_computation.239 | loop fusion | flops 193536 | bytes 442412 | tf_op jit(solution)/shard_map/add | solution.py:222
  250.9 268.0 %while.33 = (s32[]{:T(128)}, f32[3,1024]{1,0:T(4,128)S(1)}, f32[6,9,512]{2,1,0:T(8,128)}, s32[]{:T(128)}, s32[]{:T(128)}, /*index=5*/f32[6,9,512]{2,1,0:T(8,128)...) while((s32[]{:T(128)}, f32[3,1024]{1,0:T(4,128)S(1)}, ...), condition=%wide.region_26.27_spmd.clone, body=%wide.region_12.0_spmd.clone.sunk | while | flops 245467152 | bytes 84695544 | solution.py:209
  282.7 5.9 fusion.399
  288.6 9.6 %fusion.400 = f32[1024,4,128]{0,1,2:T(4,128)S(1)} fusion(f32[1024,4,128]{0,2,1:T(8,128)S(1)} %bitcast.360), kind=kOutput, calls=%fused_computation.144.clone.1 | output fusion | flops 66584576 | bytes 4194304 | tf_op jit(solution)/shard_map/reduce-window.12
  332.4 5.9 fusion.399
  338.3 9.6 %fusion.400 = f32[1024,4,128]{0,1,2:T(4,128)S(1)} fusion(f32[1024,4,128]{0,2,1:T(8,128)S(1)} %bitcast.360), kind=kOutput, calls=%fused_computation.144.clone.1 | output fusion | flops 66584576 | bytes 4194304 | tf_op jit(solution)/shard_map/reduce-window.12
  382.2 5.9 fusion.399
  388.1 9.6 %fusion.400 = f32[1024,4,128]{0,1,2:T(4,128)S(1)} fusion(f32[1024,4,128]{0,2,1:T(8,128)S(1)} %bitcast.360), kind=kOutput, calls=%fused_computation.144.clone.1 | output fusion | flops 66584576 | bytes 4194304 | tf_op jit(solution)/shard_map/reduce-window.12
  437.8 9.6 %fusion.400 = f32[1024,4,128]{0,1,2:T(4,128)S(1)} fusion(f32[1024,4,128]{0,2,1:T(8,128)S(1)} %bitcast.360), kind=kOutput, calls=%fused_computation.144.clone.1 | output fusion | flops 66584576 | bytes 4194304 | tf_op jit(solution)/shard_map/reduce-window.12
  487.5 9.6 %fusion.400 = f32[1024,4,128]{0,1,2:T(4,128)S(1)} fusion(f32[1024,4,128]{0,2,1:T(8,128)S(1)} %bitcast.360), kind=kOutput, calls=%fused_computation.144.clone.1 | output fusion | flops 66584576 | bytes 4194304 | tf_op jit(solution)/shard_map/reduce-window.12
  539.8 56.2 %all-to-all-start.2 = ((f32[8,3,59,128]{3,2,1,0:T(8,128)}), f32[8,3,59,128]{3,2,1,0:T(8,128)}, u32[]{:S(2)}, u32[]{:S(2)}) async-start(f32[8,3,59,128]{3,2,1,0:T(8,128)} %bitcast.361), calls=%async_computation.2 | async-start | bytes 1572864 | tf_op jit(solution)/shard_map/all_to_all | solution.py:329
  596.0 41.2 %psum.7 = f32[]{:T(128)} all-reduce(f32[]{:T(128)} %get-tuple-element.485), channel_id=1, replica_groups=mesh['ty'=4,'tx'=8] {'ty','tx'}, use_global_device_ids=true, to_apply=%region_32.33 | all-reduce | flops 1 | bytes 8 | tf_op jit(solution)/shard_map/psum | solution.py:318
  (565 shorter events, 350.0 us)
Async XLA Ops:
  0.6 19.4 %copy-start = (f32[96,59,128]{2,0,1:T(8,128)S(1)}, f32[96,59,128]{2,0,1:T(8,128)}, u32[]{:S(2)}) copy-start(f32[96,59,128]{2,0,1:T(8,128)} %param.13) | copy-start | bytes 8699908
  25.6 23.3 %all-to-all-start.1 = ((f32[8,3,59,128]{3,2,1,0:T(8,128)}), f32[8,3,59,128]{3,2,1,0:T(8,128)}, u32[]{:S(2)}, u32[]{:S(2)}) async-start(f32[8,3,59,128]{3,2,1,0:T(8,128)} %bitcast.367), calls=%async_computation.1 | async-start | bytes 1572864 | tf_op jit(solution)/shard_map/all_to_all | solution.py:280
  60.1 88.4 %copy-start.13 = (f32[3,32,32]{2,1,0:T(8,128)S(1)}, f32[3,32,32]{2,1,0:T(8,128)}, u32[]{:S(2)}) copy-start(f32[3,32,32]{2,1,0:T(8,128)} %param.17) | copy-start | bytes 36868
  148.4 28.0 %copy-start.20 = (f32[6,512]{1,0:T(8,128)}, f32[6,512]{1,0:T(8,128)S(1)}, u32[]{:S(2)}) copy-start(f32[6,512]{1,0:T(8,128)S(1)} %get-tuple-element.882) | copy-start | bytes 36868
  148.5 19.0 %collective-permute-start = (f32[2,3,10,32]{3,2,1,0:T(8,128)S(1)}, f32[2,3,10,32]{3,2,1,0:T(8,128)S(1)}, u32[]{:S(2)}, u32[]{:S(2)}) collective-permute-start(f32[2,3,10,32]{3,2,1,0:T(8,128)S(1)} %get-tuple-element.487), channel_id=1, source_target_pairs={{0,8},{8,16},{16,24},{1,9},{9,17},{17,25},{2,10},{10,18},{18,26},{... | collective-permute-start | bytes 23048 | tf_op jit(solution)/shard_map/ppermute | solution.py:43
  165.6 3.1 collective-permute-start.1
  169.5 9.3 %collective-permute-start.2 = (f32[2,3,52,10]{3,2,1,0:T(8,128)}, f32[2,3,52,10]{3,2,1,0:T(8,128)S(1)}, u32[]{:S(2)}, u32[]{:S(2)}) collective-permute-start(f32[2,3,52,10]{3,2,1,0:T(8,128)} %get-tuple-element.479), channel_id=1, source_target_pairs={{0,1},{1,2},{2,3},{3,4},{4,5},{5,6},{6,7},{8,9},{9,10},{10,11},{11... | collective-permute-start | bytes 37448 | tf_op jit(solution)/shard_map/ppermute | solution.py:43
  174.5 8.4 %collective-permute-start.3 = (f32[2,3,52,10]{3,2,1,0:T(8,128)}, f32[2,3,52,10]{3,2,1,0:T(8,128)}, u32[]{:S(2)}, u32[]{:S(2)}) collective-permute-start(f32[2,3,52,10]{3,2,1,0:T(8,128)} %get-tuple-element.480), channel_id=1, source_target_pairs={{1,0},{2,1},{3,2},{4,3},{5,4},{6,5},{7,6},{9,8},{10,9},{11,10},{12... | collective-permute-start | bytes 37448 | tf_op jit(solution)/shard_map/ppermute | solution.py:44
  220.1 14.5 %copy-start.34 = (f32[42,42]{1,0:T(8,128)S(1)}, f32[42,42]{1,0:T(8,128)}, u32[]{:S(2)}) copy-start(f32[42,42]{1,0:T(8,128)} %and_convert_fusion) | copy-start | bytes 21172
  234.7 16.2 %copy-start.42 = (s32[3]{0:T(128)S(1)}, s32[3]{0:T(128)}, u32[]{:S(2)}) copy-start(s32[3]{0:T(128)} %constant.235.clone.2) | copy-start | bytes 40
  518.9 12.3 %copy-start.7 = (f32[24,48,128]{2,0,1:T(8,128)S(1)}, f32[24,48,128]{2,0,1:T(8,128)}, u32[]{:S(2)}) copy-start(f32[24,48,128]{2,0,1:T(8,128)} %copy-done.6) | copy-start | bytes 1769476
  522.1 10.1 %copy-start.11 = (f32[24,1,128]{2,1,0:T(1,128)S(1)}, f32[24,1,128]{2,1,0:T(1,128)}, u32[]{:S(2)}) copy-start(f32[24,1,128]{2,1,0:T(1,128)} %copy-done.10) | copy-start | bytes 36868
  522.1 10.1 %copy-start.17 = (f32[24,1,128]{2,0,1:T(8,128)S(1)}, f32[24,1,128]{2,0,1:T(8,128)}, u32[]{:S(2)}) copy-start(f32[24,1,128]{2,0,1:T(8,128)} %get-tuple-element.502) | copy-start | bytes 36868
  522.1 10.1 %copy-start.18 = (f32[24,1,128]{2,0,1:T(8,128)S(1)}, f32[24,1,128]{2,0,1:T(8,128)}, u32[]{:S(2)}) copy-start(f32[24,1,128]{2,0,1:T(8,128)} %get-tuple-element.513) | copy-start | bytes 36868
  522.1 10.1 %copy-start.24 = (f32[24,1,128]{2,0,1:T(8,128)S(1)}, f32[24,1,128]{2,0,1:T(8,128)}, u32[]{:S(2)}) copy-start(f32[24,1,128]{2,0,1:T(8,128)} %get-tuple-element.501) | copy-start | bytes 36868
  522.1 10.2 %copy-start.25 = (f32[24,1,128]{2,0,1:T(8,128)S(1)}, f32[24,1,128]{2,0,1:T(8,128)}, u32[]{:S(2)}) copy-start(f32[24,1,128]{2,0,1:T(8,128)} %get-tuple-element.506) | copy-start | bytes 36868
  522.1 10.2 %copy-start.26 = (f32[24,1,128]{2,0,1:T(8,128)S(1)}, f32[24,1,128]{2,0,1:T(8,128)}, u32[]{:S(2)}) copy-start(f32[24,1,128]{2,0,1:T(8,128)} %get-tuple-element.507) | copy-start | bytes 36868
  522.2 10.2 %copy-start.30 = (f32[24,1,128]{2,0,1:T(8,128)S(1)}, f32[24,1,128]{2,0,1:T(8,128)}, u32[]{:S(2)}) copy-start(f32[24,1,128]{2,0,1:T(8,128)} %get-tuple-element.503) | copy-start | bytes 36868
  522.2 10.2 %copy-start.31 = (f32[24,1,128]{2,0,1:T(8,128)S(1)}, f32[24,1,128]{2,0,1:T(8,128)}, u32[]{:S(2)}) copy-start(f32[24,1,128]{2,0,1:T(8,128)} %get-tuple-element.504) | copy-start | bytes 36868
  522.2 10.2 %copy-start.32 = (f32[24,1,128]{2,0,1:T(8,128)S(1)}, f32[24,1,128]{2,0,1:T(8,128)}, u32[]{:S(2)}) copy-start(f32[24,1,128]{2,0,1:T(8,128)} %get-tuple-element.516) | copy-start | bytes 36868
  522.2 10.2 %copy-start.33 = (f32[24,1,128]{2,0,1:T(8,128)S(1)}, f32[24,1,128]{2,0,1:T(8,128)}, u32[]{:S(2)}) copy-start(f32[24,1,128]{2,0,1:T(8,128)} %get-tuple-element.519) | copy-start | bytes 36868
  522.2 10.2 %copy-start.41 = (f32[24,1,128]{2,0,1:T(8,128)S(1)}, f32[24,1,128]{2,0,1:T(8,128)}, u32[]{:S(2)}) copy-start(f32[24,1,128]{2,0,1:T(8,128)} %get-tuple-element.499) | copy-start | bytes 36868
  539.8 100.1 %copy-start.46 = (s32[24]{0:T(128)S(1)}, s32[24]{0:T(128)}, u32[]{:S(2)}) copy-start(s32[24]{0:T(128)} %get-tuple-element.546) | copy-start | bytes 292
  539.8 98.1 %all-to-all-start.2 = ((f32[8,3,59,128]{3,2,1,0:T(8,128)}), f32[8,3,59,128]{3,2,1,0:T(8,128)}, u32[]{:S(2)}, u32[]{:S(2)}) async-start(f32[8,3,59,128]{3,2,1,0:T(8,128)} %bitcast.361), calls=%async_computation.2 | async-start | bytes 1572864 | tf_op jit(solution)/shard_map/all_to_all | solution.py:329
  (49 other events, 155.2 us)
where the time goes:
time: 662 us; the launch traced here: 652 us
  other arithmetic  301 us (45%)
  local copies, waits for them, and re-layouts  99.5 us (15%)
  starting transfers between devices  85 us (13%)
  matrix products  61.6 us (9%)
  blocking collectives  54.8 us (8%)
  waiting for transfers between devices  25.1 us (4%)
  loops' own time  20.8 us (3%)
    another operation x61, other arithmetic  124 us
    dot_general x20, matrix products, composite(): jnp.dot(flat[6:9], weight, precision=lax.Precision.HIGHEST, preferred_ele...  61.6 us
    all_to_all x1, starting transfers between devices, per_device(): lax.all_to_all(reply.reshape(across, capacity, fields, block), 'tx', spli...  56.2 us
    add x6, other arithmetic, filtered(): sum((taps[shift] * field[..., :, shift:shift + cols] for shift in range(1...  43.7 us
    psum x1, blocking collectives, per_device(): total = lax.psum(local_total, ('ty', 'tx'))  41.2 us
    reduce_sum x10, other arithmetic, composite(): return (color, jnp.sum(keep, axis=0))  26.6 us
    another operation x48, local copies, waits for them, and re-layouts  25.9 us
    mul x30, other arithmetic, composite(): alpha = (live * flat[5])[:, None] * jnp.exp(-0.5 * power)  25.3 us
  transfers between devices with their start and end apart: 6, of which 4 were waited for; matrix products, arithmetic and copies ran while one was open for 0% of the time, Pallas kernels for 0%

commit v1 on v0

v1 whole, which is shorter than its diff:
```python
import functools

import jax
import jax.numpy as jnp
import ml_dtypes
import numpy as np
from jax import lax
from jax.experimental import pallas as pl
from jax.experimental.pallas import tpu as pltpu
from jax.sharding import PartitionSpec as P

CAP = 3
SEGS = 8
LANES = 128
CHUNK = 128
STEPS = CHUNK // SEGS
RIM = 5
TAPS = 2 * RIM + 1
LOG2E = 1.4426950408889634
LN2 = 0.6931471805599453
DARK = -1e30

FOCAL = 1000.0
LOW_PASS = 0.3
STRUCT_WEIGHT = 0.2
LUMA_TERM = 0.0001
CONTRAST_TERM = 0.0009
ROBUST_TERM = 1e-06
HARMONIC_ZERO = 0.28209479177387814
HARMONIC_ONE = 0.4886025119029199
HARMONIC_TWO = (
    1.0925484305920792,
    -1.0925484305920792,
    0.31539156525252005,
    -1.0925484305920792,
    0.5462742152960396,
)
HARMONIC_THREE = (
    -0.5900435899266435,
    2.890611442640554,
    -0.4570457994644658,
    0.3731763325901154,
    -0.4570457994644658,
    1.445305721320277,
    -0.5900435899266435,
)

HIGH = lax.Precision.HIGHEST
F32 = jnp.float32
BF16 = jnp.bfloat16
ANY = pl.BlockSpec(memory_space=pl.ANY)
SMEM = pl.BlockSpec(memory_space=pltpu.SMEM)
VMEM = pl.BlockSpec(memory_space=pltpu.VMEM)
PARAMS = pltpu.CompilerParams(vmem_limit_bytes=56 * 1024 * 1024)


def harmonics(x, y, z):
    xx, yy, zz = x * x, y * y, z * z
    xy, yz, xz = x * y, y * z, x * z
    return [
        HARMONIC_ZERO * jnp.ones_like(x),
        -HARMONIC_ONE * y,
        HARMONIC_ONE * z,
        -HARMONIC_ONE * x,
        HARMONIC_TWO[0] * xy,
        HARMONIC_TWO[1] * yz,
        HARMONIC_TWO[2] * (2.0 * zz - xx - yy),
        HARMONIC_TWO[3] * xz,
        HARMONIC_TWO[4] * (xx - yy),
        HARMONIC_THREE[0] * y * (3.0 * xx - yy),
        HARMONIC_THREE[1] * xy * z,
        HARMONIC_THREE[2] * y * (4.0 * zz - xx - yy),
        HARMONIC_THREE[3] * z * (2.0 * zz - 3.0 * xx - 3.0 * yy),
        HARMONIC_THREE[4] * x * (4.0 * zz - xx - yy),
        HARMONIC_THREE[5] * z * (xx - yy),
        HARMONIC_THREE[6] * x * (xx - 3.0 * yy),
    ]


def directions(x, y, z):
    length = jnp.sqrt(x * x + y * y + z * z)
    return harmonics(x / length, y / length, z / length)


def exponent(mean_x, mean_y, mean_z, log_scale, quat, log_opacity, shift_x, shift_y):
    scale = [jnp.exp(s) for s in log_scale]
    norm = jnp.sqrt(quat[0] * quat[0] + quat[1] * quat[1] + quat[2] * quat[2] + quat[3] * quat[3])
    w, i, j, k = (q / norm for q in quat)
    rotation = [
        [1.0 - 2.0 * (j * j + k * k), 2.0 * (i * j - w * k), 2.0 * (i * k + w * j)],
        [2.0 * (i * j + w * k), 1.0 - 2.0 * (i * i + k * k), 2.0 * (j * k - w * i)],
        [2.0 * (i * k - w * j), 2.0 * (j * k + w * i), 1.0 - 2.0 * (i * i + j * j)],
    ]
    scaled = [[rotation[r][c] * scale[c] for c in range(3)] for r in range(3)]

    def sigma(r, c):
        return scaled[r][0] * scaled[c][0] + scaled[r][1] * scaled[c][1] + scaled[r][2] * scaled[c][2]

    s00, s01, s02, s11, s12, s22 = (
        sigma(0, 0), sigma(0, 1), sigma(0, 2), sigma(1, 1), sigma(1, 2), sigma(2, 2),
    )
    inverse_z = 1.0 / mean_z
    diag = FOCAL * inverse_z
    jac_xz = -FOCAL * mean_x * inverse_z * inverse_z
    jac_yz = -FOCAL * mean_y * inverse_z * inverse_z
    u0, u1, u2 = diag * s00 + jac_xz * s02, diag * s01 + jac_xz * s12, diag * s02 + jac_xz * s22
    v1, v2 = diag * s11 + jac_yz * s12, diag * s12 + jac_yz * s22
    cov_uu = u0 * diag + u2 * jac_xz + LOW_PASS
    cov_uv = u1 * diag + u2 * jac_yz
    cov_vv = v1 * diag + v2 * jac_yz + LOW_PASS
    determinant = cov_uu * cov_vv - cov_uv * cov_uv
    pos_u = FOCAL * mean_x * inverse_z + shift_x
    pos_v = FOCAL * mean_y * inverse_z + shift_y
    half = -0.5 * LOG2E
    xx = half * (cov_vv / determinant)
    xy = (-2.0 * half) * (cov_uv / determinant)
    yy = half * (cov_uu / determinant)
    x1 = -2.0 * xx * pos_u - xy * pos_v
    y1 = -2.0 * yy * pos_v - xy * pos_u
    one = xx * pos_u * pos_u + xy * pos_u * pos_v + yy * pos_v * pos_v + log_opacity
    return xx, xy, yy, x1, y1, one


def tile_shifts(across, side, height, width):
    column = lax.broadcasted_iota(jnp.int32, (across, LANES), 0).astype(F32)
    column = jnp.concatenate([column] * CAP, axis=0)
    row = lax.axis_index("ty").astype(F32)
    shift_x = (0.5 * width - 0.5 * side - 0.5) - side * column
    shift_y = jnp.full(column.shape, (0.5 * height - 0.5 * side - 0.5) - side * row, F32)
    return shift_x, shift_y


def request_kernel(owned, across, lists, count, order, request, slot, seen):
    base = lax.axis_index("ty") * across
    for o in range(across):
        seen[o] = 0
        for c in range(CAP):
            request[o * CAP + c] = -1
    used = count[0, 0]

    def entry(k, _):
        @pl.when(k < used)
        def _():
            block = order[lists[0, 0, k]]
            home = block // owned
            local = block - home * owned
            home = home - base
            at = seen[home]
            seen[home] = at + 1
            request[home * CAP + at] = local
            slot[k] = home * CAP + at

        @pl.when(k >= used)
        def _():
            slot[k] = -1

        return 0

    lax.fori_loop(0, slot.shape[0], entry, 0)


def serve_kernel(across, side, height, width, asked, gaussians, send, raw, empty, zeros, in_sem, zero_sem):
    slots = across * CAP
    for s in range(slots):
        c, t = divmod(s, across)
        index = jnp.maximum(asked[t * CAP + c], 0)
        pltpu.make_async_copy(gaussians.at[index], raw.at[s], in_sem.at[s]).start()
    zeros[...] = jnp.zeros_like(zeros)
    span = zeros.shape[0]
    fills = empty.shape[0] // span
    for n in range(fills):
        pltpu.make_async_copy(zeros, empty.at[pl.ds(n * span, span)], zero_sem.at[n]).start()
    for s in range(slots):
        pltpu.make_async_copy(gaussians.at[0], raw.at[s], in_sem.at[s]).wait()
    field = [raw[:, f, :] for f in range(11)]
    shift_x, shift_y = tile_shifts(across, side, height, width)
    light = -LOG2E * jnp.log(1.0 + jnp.exp(-field[10])) + float(np.log2(0.99))
    light = jnp.maximum(light, DARK)
    rows = list(
        exponent(field[0], field[1], field[2], field[3:6], field[6:10], light, shift_x, shift_y)
    )
    basis = directions(field[0], field[1], field[2])
    for ch in range(3):
        color = 0.5 + basis[0] * raw[:, 11 + ch, :]
        for m in range(1, 16):
            color = color + basis[m] * raw[:, 11 + 3 * m + ch, :]
        rows.append(color)
    for c in range(CAP):
        for f in range(9):
            at = c * 8 + f if f < 8 else CAP * 8 + c
            send[:, at, :] = rows[f][c * across : (c + 1) * across]
    for n in range(fills):
        pltpu.make_async_copy(zeros, empty.at[pl.ds(n * span, span)], zero_sem.at[n]).wait()


def repeated(x, times):
    return jnp.concatenate([x] * times, axis=1)


def forward_kernel(
    slot, recv, planes, target, table, checks, prefix, behind, dense, spread, buf_a, buf_b, ends
):
    lmax = slot.shape[0]
    per = lmax // SEGS
    pixels = prefix.shape[1]
    groups = pixels // LANES
    zero_rows = jnp.zeros((7, LANES), F32)
    dead = jnp.where(lax.broadcasted_iota(jnp.int32, (16, LANES), 0) == 5, DARK, 0.0)
    is_color = lax.broadcasted_iota(jnp.int32, (16, LANES), 0) >= 6
    filler = jnp.zeros((LANES - 48, LANES), F32)

    def place(k, _):
        s = slot[k]
        live = s >= 0
        s = jnp.maximum(s, 0)
        o = s // CAP
        c = s - o * CAP
        head = recv[o, pl.ds(pl.multiple_of(c * 8, 8), 8), :]
        tail = recv[o, pl.ds(CAP * 8 + c, 1), :]
        rows = jnp.concatenate([head, tail, zero_rows], axis=0)
        rows = jnp.where(live, rows, dead)
        hi = rows.astype(BF16).astype(F32)
        rest = rows - hi
        mid = rest.astype(BF16).astype(F32)
        low = (rest - mid).astype(BF16).astype(F32)
        third = jnp.where(is_color, hi, low)
        stacked = jnp.concatenate([hi, mid, third, filler], axis=0)
        seg = k // per
        m = k - seg * per
        spread[pl.ds(m * (SEGS * LANES) + seg, LANES, stride=SEGS), :] = stacked.T
        return 0

    lax.fori_loop(0, lmax, place, 0)

    def products(n, buf):
        part = spread[pl.ds(pl.multiple_of(n * CHUNK, CHUNK), CHUNK), :].astype(BF16)
        table[pl.ds(pl.multiple_of(n * CHUNK, CHUNK), CHUNK), :] = part
        buf[...] = jnp.dot(part, planes[...], preferred_element_type=F32)

    def blend(n, buf, carry):
        light, red, green, blue = carry
        checks[n] = light
        for i in range(STEPS):
            rows = pl.ds(i * SEGS, SEGS)
            weight = light * jnp.exp2(buf[rows, :pixels])
            light = light - weight
            red = red + weight * repeated(buf[rows, pixels : pixels + LANES], groups)
            green = green + weight * repeated(buf[rows, pixels + LANES : pixels + 2 * LANES], groups)
            blue = blue + weight * repeated(
                buf[rows, pixels + 2 * LANES : pixels + 3 * LANES], groups
            )
        return light, red, green, blue

    products(0, buf_a)
    chunks = lmax * LANES // CHUNK

    def pair(h, carry):
        n = 2 * h
        products(n + 1, buf_b)
        carry = blend(n, buf_a, carry)
        products(jnp.minimum(n + 2, chunks - 1), buf_a)
        return blend(n + 1, buf_b, carry)

    start = (jnp.ones((SEGS, pixels), F32),) + (jnp.zeros((SEGS, pixels), F32),) * 3
    carry = lax.fori_loop(0, chunks // 2, pair, start)
    for f in range(4):
        ends[f] = carry[f]
    ahead = jnp.ones((1, pixels), F32)
    for seg in range(SEGS):
        prefix[pl.ds(seg, 1), :] = ahead
        ahead = ahead * ends[0, pl.ds(seg, 1), :]
    for ch in range(3):
        seen = jnp.zeros((1, pixels), F32)
        for seg in reversed(range(SEGS)):
            behind[ch, pl.ds(seg, 1), :] = seen
            seen = ends[1 + ch, pl.ds(seg, 1), :] + ends[0, pl.ds(seg, 1), :] * seen
        for j in range(groups):
            dense[pl.ds(ch * groups + j, 1), :] = seen[:, j * LANES : (j + 1) * LANES]
    dense[3 * groups :, :] = target[...]


def similarity(mean_a, mean_b, square_a, square_b, cross):
    var_a = square_a - mean_a * mean_a
    var_b = square_b - mean_b * mean_b
    covar = cross - mean_a * mean_b
    top = (2.0 * mean_a * mean_b + LUMA_TERM) * (2.0 * covar + CONTRAST_TERM)
    bottom = (mean_a * mean_a + mean_b * mean_b + LUMA_TERM) * (var_a + var_b + CONTRAST_TERM)
    return top / bottom


def score_kernel(side, height, width, near, fa, fb, fc, fd, slope, loss):
    rows3 = near[0].shape[0] // 2
    groups = rows3 // 3
    fold = LANES // side
    fields = [[], [], [], [], []]
    for v in range(3):
        strip = jnp.concatenate([near[3 * v + h][...] for h in range(3)], axis=1)
        image, target = strip[:rows3], strip[rows3:]
        for f, plane in enumerate([image, target, image * image, target * target, image * target]):
            fields[f].append(plane)
    stack = jnp.concatenate([fields[f][v] for f in range(5) for v in range(3)], axis=0)
    wide = jnp.dot(stack, fa[...], precision=HIGH, preferred_element_type=F32)
    columns = []
    for f in range(5):
        for ch in range(3):
            parts = []
            for t in range(fold):
                for v in range(3):
                    at = (f * 3 + v) * rows3 + ch * groups
                    parts.append(wide[at : at + groups, t * LANES : (t + 1) * LANES])
            columns.append(jnp.concatenate(parts, axis=0))
    tall = jnp.concatenate(columns, axis=1)
    maps = jnp.dot(fb[...], tall, precision=HIGH, preferred_element_type=F32)
    span = 3 * LANES
    score, pull = jax.vjp(similarity, *[maps[:, f * span : (f + 1) * span] for f in range(5)])
    parts = pull(jnp.full(score.shape, -STRUCT_WEIGHT, F32))
    row = lax.broadcasted_iota(jnp.int32, score.shape, 0)
    col = lax.broadcasted_iota(jnp.int32, (score.shape[0], LANES), 1)
    col = jnp.concatenate([col] * 3, axis=1)
    row_at = row - RIM + lax.axis_index("ty") * side
    col_at = col - RIM + lax.axis_index("tx") * side
    reach = side + 2 * RIM
    inside = (
        (row_at >= 0) & (row_at < height) & (col_at >= 0) & (col_at < width)
        & (row < reach) & (col < reach)
    )
    own = (row >= RIM) & (row < RIM + side) & (col >= RIM) & (col < RIM + side)
    coeffs = jnp.concatenate(
        [jnp.where(inside, parts[f], 0.0) for f in (0, 2, 4)], axis=1
    )
    low = jnp.dot(fc[...], coeffs, precision=HIGH, preferred_element_type=F32)
    rows = []
    for n in range(9):
        rows.append(
            jnp.concatenate(
                [
                    low[t * groups : (t + 1) * groups, n * LANES : (n + 1) * LANES]
                    for t in range(fold)
                ],
                axis=1,
            )
        )
    smooth = jnp.dot(
        jnp.concatenate(rows, axis=0), fd[...], precision=HIGH, preferred_element_type=F32
    )
    image, target = near[4][:rows3, :], near[4][rows3:, :]
    gap = image - target
    robust = jnp.sqrt(gap * gap + ROBUST_TERM)
    slope[...] = (
        smooth[:rows3]
        + 2.0 * image * smooth[rows3 : 2 * rows3]
        + target * smooth[2 * rows3 :]
        + (1.0 - STRUCT_WEIGHT) * gap / robust
    )
    total = (1.0 - STRUCT_WEIGHT) * jnp.sum(robust) + STRUCT_WEIGHT * jnp.sum(
        jnp.where(own, 1.0 - score, 0.0)
    )
    loss[0] = total


def score_entry(side, height, width, *refs):
    score_kernel(side, height, width, refs[:9], *refs[9:])


def backward_kernel(
    slot, table, checks, prefix, behind, slope, planes, reduce, reply,
    rhs, wide, grows, buf_a, buf_b, weights, alphas, sums, moments,
):
    lmax = slot.shape[0]
    per = lmax // SEGS
    pixels = prefix.shape[1]
    groups = pixels // LANES
    chunks = lmax * LANES // CHUNK
    wide[...] = jnp.zeros_like(wide)
    for ch in range(3):
        for j in range(groups):
            lanes = pl.ds(j * LANES, LANES)
            wide[pl.ds(6 + ch, 1), lanes] = slope[pl.ds(ch * groups + j, 1), :]
    for ch in range(3):
        row = wide[pl.ds(6 + ch, 1), :]
        hi = row.astype(BF16).astype(F32)
        grows[ch] = jnp.broadcast_to(row, (SEGS, pixels))
        wide[pl.ds(6 + ch, 1), :] = hi
        wide[pl.ds(22 + ch, 1), :] = hi
        wide[pl.ds(38 + ch, 1), :] = row - hi
    rhs[:, :pixels] = planes[:, :pixels]
    rhs[:, pixels:] = wide[...].astype(BF16)

    def products(n, buf):
        part = table[pl.ds(pl.multiple_of(n * CHUNK, CHUNK), CHUNK), :]
        buf[...] = jnp.dot(part, rhs[...], preferred_element_type=F32)

    def sweep(n, buf, back):
        light = checks[n] * prefix[...]
        for i in range(STEPS):
            rows = pl.ds(i * SEGS, SEGS)
            alpha = jnp.exp2(buf[rows, :pixels])
            weight = light * alpha
            light = light - weight
            weights[rows, :] = weight
            alphas[rows, :] = alpha
        for i in reversed(range(STEPS)):
            rows = pl.ds(i * SEGS, SEGS)
            weight = weights[rows, :]
            gap = buf[rows, pixels:] - back
            back = back + alphas[rows, :] * gap
            pull = weight * gap
            zero = one = two = None
            for j in reversed(range(groups)):
                piece = pull[:, j * LANES : (j + 1) * LANES]
                zero = piece if zero is None else zero + piece
                if j > 0:
                    one = zero if one is None else one + zero
                    two = one if two is None else two + one
            sums[rows, 0:LANES] = zero
            sums[rows, LANES : 2 * LANES] = one
            sums[rows, 2 * LANES : 3 * LANES] = two
            for ch in range(3):
                tint = weight * grows[ch]
                total = tint[:, :LANES]
                for j in range(1, groups):
                    total = total + tint[:, j * LANES : (j + 1) * LANES]
                sums[rows, (3 + ch) * LANES : (4 + ch) * LANES] = total
        whole = sums[...]
        hi = whole.astype(BF16)
        low = (whole - hi.astype(F32)).astype(BF16)
        moments[pl.ds(pl.multiple_of(n * CHUNK, CHUNK), CHUNK), :] = jnp.dot(
            hi, reduce[...], preferred_element_type=F32
        ) + jnp.dot(low, reduce[...], preferred_element_type=F32)
        return back

    back = behind[0] * grows[0] + behind[1] * grows[1] + behind[2] * grows[2]
    products(chunks - 1, buf_a)

    def pair(h, back):
        n = chunks - 1 - 2 * h
        products(n - 1, buf_b)
        back = sweep(n, buf_a, back)
        products(jnp.maximum(n - 2, 0), buf_a)
        return sweep(n - 1, buf_b, back)

    lax.fori_loop(0, chunks // 2, pair, back)

    def collect(k, _):
        s = slot[k]

        @pl.when(s >= 0)
        def _():
            o = s // CAP
            c = s - o * CAP
            seg = k // per
            m = k - seg * per
            block = moments[pl.ds(m * (SEGS * LANES) + seg, LANES, stride=SEGS), :].T
            reply[o, pl.ds(pl.multiple_of(c * 8, 8), 8), :] = block[:8]
            reply[o, pl.ds(CAP * 8 + c, 1), :] = block[8:9]

        return 0

    lax.fori_loop(0, lmax, collect, 0)


def gather_kernel(across, side, height, width, asked, got, raw, empty, grads, pieces, sem):
    slots = across * CAP
    field = [raw[:, f, :] for f in range(11)]
    shift_x, shift_y = tile_shifts(across, side, height, width)

    def received(f):
        at = [c * 8 + f if f < 8 else CAP * 8 + c for c in range(CAP)]
        return jnp.concatenate([got[:, a, :] for a in at], axis=0)

    def shaped(x, y, z, log_scale, quat):
        light = jnp.zeros_like(x)
        return exponent(x, y, z, log_scale, quat, light, shift_x, shift_y)

    _, pull = jax.vjp(shaped, *field[:3], field[3:6], field[6:10])
    moments = [LN2 * received(f) for f in range(6)]
    gx, gy, gz, gscale, gquat = pull(tuple(moments))
    basis, pull_basis = jax.vjp(directions, *field[:3])
    tints = [received(6 + ch) for ch in range(3)]
    tilts = []
    for m in range(16):
        tilt = None
        for ch in range(3):
            term = tints[ch] * raw[:, 11 + 3 * m + ch, :]
            tilt = term if tilt is None else tilt + term
            pieces[:, 11 + 3 * m + ch, :] = tints[ch] * basis[m]
        tilts.append(tilt)
    dx, dy, dz = pull_basis(tilts)
    pieces[:, 0, :] = gx + dx
    pieces[:, 1, :] = gy + dy
    pieces[:, 2, :] = gz + dz
    for f in range(3):
        pieces[:, 3 + f, :] = gscale[f]
    for f in range(4):
        pieces[:, 6 + f, :] = gquat[f]
    pieces[:, 10, :] = moments[5] * (LOG2E / (1.0 + jnp.exp(field[10])))

    for s in range(slots):
        c, t = divmod(s, across)
        index = asked[t * CAP + c]

        @pl.when(index >= 0)
        def _():
            pltpu.make_async_copy(pieces.at[s], grads.at[index], sem.at[s]).start()

    for s in range(slots):
        c, t = divmod(s, across)
        index = asked[t * CAP + c]

        @pl.when(index >= 0)
        def _():
            pltpu.make_async_copy(pieces.at[s], grads.at[index], sem.at[s]).wait()


def tile_planes(side):
    pixel = np.arange(side * side)
    x = (pixel % side - side // 2).astype(np.float64)
    y = (pixel // side - side // 2).astype(np.float64)
    mono = np.stack([x * x, x * y, y * y, x, y, np.ones_like(x)])
    table = np.zeros((LANES, side * side + 3 * LANES))
    for g in range(3):
        table[16 * g : 16 * g + 6, : side * side] = mono
    for ch in range(3):
        at = side * side + ch * LANES
        table[6 + ch, at : at + LANES] = 1.0
        table[22 + ch, at : at + LANES] = 1.0
    return table.astype(ml_dtypes.bfloat16)


def moment_columns(side):
    lane = np.arange(LANES)
    x = lane % side - side // 2
    t = lane // side - side // 2
    step = LANES // side
    one = np.ones_like(x)
    out = np.zeros((6 * LANES, LANES))
    out[:LANES, :6] = np.stack([x * x, x * t, t * t, x, t, one], axis=1)
    out[LANES : 2 * LANES, 1] = step * x
    out[LANES : 2 * LANES, 2] = 2 * step * t - step * step
    out[LANES : 2 * LANES, 4] = step
    out[2 * LANES : 3 * LANES, 2] = 2 * step * step
    for ch in range(3):
        out[(3 + ch) * LANES : (4 + ch) * LANES, 6 + ch] = 1.0
    return out.astype(ml_dtypes.bfloat16)


def filters(side):
    offsets = np.arange(TAPS) - float(RIM)
    taps = np.exp(-offsets * offsets / 4.5)
    taps = taps / taps.sum()
    reach = side + 2 * RIM
    padded = -(-reach // 8) * 8
    fold = LANES // side
    groups = side // fold

    def tap(distance):
        at = distance + RIM
        return np.where((at >= 0) & (at < TAPS), taps[np.clip(at, 0, TAPS - 1)], 0.0)

    out = np.arange(reach) - RIM
    source = np.arange(-side, 2 * side)
    along = tap(source[:, None] - out[None, :])
    fa = np.zeros((3, fold, side, fold, LANES))
    for t in range(fold):
        fa[:, t, :, t, :reach] = along.reshape(3, side, reach)
    fa = fa.reshape(3 * LANES, fold * LANES)
    fb = np.zeros((padded, fold, 3, groups))
    fb[:reach] = along.reshape(3, groups, fold, reach).transpose(3, 2, 0, 1)
    fb = fb.reshape(padded, fold * 3 * groups)
    inner = np.arange(side)
    back = tap(out[:, None] - inner[None, :])
    fc = np.zeros((fold, groups, padded))
    fc[:, :, :reach] = back.reshape(reach, groups, fold).transpose(2, 1, 0)
    fc = fc.reshape(fold * groups, padded)
    fd = np.zeros((fold, LANES, fold, side))
    for t in range(fold):
        fd[t, :reach, t, :] = back
    fd = fd.reshape(fold * LANES, LANES)
    return [m.astype(np.float32) for m in (fa, fb, fc, fd)]


def neighbours(x):
    down, across = lax.axis_size("ty"), lax.axis_size("tx")
    out = []
    for dv in (-1, 0, 1):
        for dh in (-1, 0, 1):
            if dv == 0 and dh == 0:
                out.append(x)
                continue
            pairs = [
                ((r + dv) * across + c + dh, r * across + c)
                for r in range(down)
                for c in range(across)
                if 0 <= r + dv < down and 0 <= c + dh < across
            ]
            out.append(lax.ppermute(x, ("ty", "tx"), pairs))
    return out


def per_device(gaussians, tile_lists, tile_counts, depth_order, target):
    owned, fields, block = gaussians.shape
    lmax = tile_lists.shape[2]
    side = target.shape[1]
    pixels = side * side
    groups = pixels // LANES
    across = lax.axis_size("tx")
    height = side * lax.axis_size("ty")
    width = side * across
    slots = across * CAP
    depth = -(-CAP * 9 // 8) * 8
    f32 = functools.partial(jax.ShapeDtypeStruct, dtype=F32)
    i32 = functools.partial(jax.ShapeDtypeStruct, dtype=jnp.int32)
    planes = jnp.asarray(tile_planes(side))
    reduce = jnp.asarray(moment_columns(side))
    bands = [jnp.asarray(m) for m in filters(side)]

    request, slot = pl.pallas_call(
        functools.partial(request_kernel, owned, across),
        out_shape=(i32((slots,)), i32((lmax,))),
        in_specs=[SMEM] * 3,
        out_specs=(SMEM, SMEM),
        scratch_shapes=[pltpu.SMEM((across,), jnp.int32)],
        name="request",
    )(tile_lists, tile_counts, depth_order)
    asked = lax.all_to_all(
        request.reshape(across, CAP), "tx", split_axis=0, concat_axis=0, tiled=True
    ).reshape(slots)
    span = 8
    send, raw, empty = pl.pallas_call(
        functools.partial(serve_kernel, across, side, float(height), float(width)),
        out_shape=(f32((across, depth, block)), f32((slots, fields, block)), f32(gaussians.shape)),
        in_specs=[SMEM, ANY],
        out_specs=(VMEM, VMEM, ANY),
        scratch_shapes=[
            pltpu.VMEM((span, fields, block), F32),
            pltpu.SemaphoreType.DMA((slots,)),
            pltpu.SemaphoreType.DMA((owned // span,)),
        ],
        compiler_params=PARAMS,
        name="serve",
    )(asked, gaussians)
    recv = lax.all_to_all(send, "tx", split_axis=0, concat_axis=0, tiled=True)
    chunks = lmax * block // CHUNK
    wide = pixels + 3 * LANES
    table, checks, prefix, behind, dense = pl.pallas_call(
        forward_kernel,
        out_shape=(
            jax.ShapeDtypeStruct((lmax * block, LANES), BF16),
            f32((chunks, SEGS, pixels)),
            f32((SEGS, pixels)),
            f32((3, SEGS, pixels)),
            f32((6 * groups, LANES)),
        ),
        in_specs=[SMEM, VMEM, VMEM, VMEM],
        out_specs=(VMEM,) * 5,
        scratch_shapes=[
            pltpu.VMEM((lmax * block, LANES), F32),
            pltpu.VMEM((CHUNK, wide), F32),
            pltpu.VMEM((CHUNK, wide), F32),
            pltpu.VMEM((4, SEGS, pixels), F32),
        ],
        compiler_params=PARAMS,
        name="forward",
    )(slot, recv, planes, target.reshape(3 * groups, LANES))
    near = neighbours(dense)
    slope, part = pl.pallas_call(
        functools.partial(score_entry, side, height, width),
        out_shape=(f32((3 * groups, LANES)), f32((1,))),
        in_specs=[VMEM] * 13,
        out_specs=(VMEM, SMEM),
        compiler_params=PARAMS,
        name="score",
    )(*near, *bands)
    total = lax.psum(part[0], ("ty", "tx"))
    reply = pl.pallas_call(
        backward_kernel,
        out_shape=f32((across, depth, block)),
        in_specs=[SMEM] + [VMEM] * 7,
        out_specs=VMEM,
        scratch_shapes=[
            pltpu.VMEM((LANES, 2 * pixels), BF16),
            pltpu.VMEM((LANES, pixels), F32),
            pltpu.VMEM((3, SEGS, pixels), F32),
            pltpu.VMEM((CHUNK, 2 * pixels), F32),
            pltpu.VMEM((CHUNK, 2 * pixels), F32),
            pltpu.VMEM((CHUNK, pixels), F32),
            pltpu.VMEM((CHUNK, pixels), F32),
            pltpu.VMEM((CHUNK, 6 * LANES), F32),
            pltpu.VMEM((lmax * block, LANES), F32),
        ],
        compiler_params=PARAMS,
        name="backward",
    )(slot, table, checks, prefix, behind, slope, planes, reduce)
    got = lax.all_to_all(reply, "tx", split_axis=0, concat_axis=0, tiled=True)
    grads = pl.pallas_call(
        functools.partial(gather_kernel, across, side, float(height), float(width)),
        out_shape=f32(gaussians.shape),
        in_specs=[SMEM, VMEM, VMEM, ANY],
        out_specs=ANY,
        scratch_shapes=[
            pltpu.VMEM((slots, fields, block), F32),
            pltpu.SemaphoreType.DMA((slots,)),
        ],
        input_output_aliases={3: 0},
        compiler_params=PARAMS,
        name="gather",
    )(asked, got, raw, empty)
    return (grads, total / (3.0 * height * width))


def solution(mesh):
    return jax.shard_map(
        per_device,
        mesh=mesh,
        in_specs=(
            P(("ty", "tx"), None, None),
            P("ty", "tx", None),
            P("ty", "tx"),
            P(),
            P(None, "ty", "tx"),
        ),
        out_specs=(P(("ty", "tx"), None, None), P()),
        check_vma=False,
    )
```

time: 662 us -> 155 us (0.23); the launches traced: 652 us -> 154 us
  other arithmetic: 301 us -> 0.66 us
  local copies, waits for them, and re-layouts: 99.5 us -> 15.4 us
  matrix products: 61.6 us -> 0 us
  starting transfers between devices: 85 us -> 30.5 us
  Pallas kernels: 0 us -> 43.5 us
  loops' own time: 20.8 us -> 0 us
  blocking collectives: 54.8 us -> 43.4 us
  waiting for transfers between devices: 25.1 us -> 17.3 us
    another operation x65 -> x0, other arithmetic: 124 us -> none
    dot_general x20 -> x0, matrix products: 61.6 us -> none  [composite(): jnp.dot(flat[6:9], weight, precision=lax.Precision.HIGHEST, preferred_ele...]
    add x23 -> x0, other arithmetic: 50.9 us -> none  [the longest x6 43.7 us: filtered(): sum((taps[shift] * field[..., :, shift:shift + cols] for shift in range(1...]
    reduce_sum x26 -> x0, other arithmetic: 47.2 us -> none  [the longest x10 26.6 us: composite(): return (color, jnp.sum(keep, axis=0))]
    all_to_all x2 -> x3, starting transfers between devices: 60.4 us -> 15.5 us  [the longest x1 7.28 us: per_device(): lax.all_to_all(request.reshape(across, CAP), 'tx', split_axis=0, concat_a...]
    mul x54 -> x0, other arithmetic: 43.9 us -> none  [the longest x30 25.3 us: composite(): alpha = (live * flat[5])[:, None] * jnp.exp(-0.5 * power)]
    pallas_call x0 -> x6, Pallas kernels: none -> 43.5 us  [the longest x1 15.9 us: per_device(): pl.pallas_call(backward_kernel, out_shape=f32((across, depth, block)), in...]
    another operation x50 -> x0, local copies, waits for them, and re-layouts: 27.4 us -> none
  transfers between devices with their start and end apart: 6 -> 11, of which waited for: 4 -> 5; matrix products, arithmetic and copies ran while one was open for 0% -> 4% of each run, Pallas kernels for 0% -> 0%
where the time goes in v1:
time: 155 us; the launch traced here: 154 us
  Pallas kernels  43.5 us (28%)
  blocking collectives  43.4 us (28%)
  starting transfers between devices  30.5 us (20%)
  waiting for transfers between devices  17.3 us (11%)
  local copies, waits for them, and re-layouts  15.4 us (10%)
  between operations  3.31 us (2%)
    psum x1, blocking collectives, per_device(): total = lax.psum(part[0], ('ty', 'tx'))  43.4 us
    pallas_call x1, Pallas kernels, per_device(): pl.pallas_call(backward_kernel, out_shape=f32((across, depth, block)), in...  15.9 us
    ppermute x8, starting transfers between devices, neighbours(): out.append(lax.ppermute(x, ('ty', 'tx'), pairs))  15 us
    unnamed x24, local copies, waits for them, and re-layouts  12.2 us
    pallas_call x1, Pallas kernels, per_device(): pl.pallas_call(forward_kernel, out_shape=(jax.ShapeDtypeStruct((lmax * bl...  11.3 us
    ppermute x8, waiting for transfers between devices, neighbours(): out.append(lax.ppermute(x, ('ty', 'tx'), pairs))  9.45 us
    all_to_all x1, starting transfers between devices, per_device(): lax.all_to_all(request.reshape(across, CAP), 'tx', split_axis=0, concat_a...  7.28 us
    all_to_all x1, waiting for transfers between devices, per_device(): recv = lax.all_to_all(send, 'tx', split_axis=0, concat_axis=0, tiled=True)  6.67 us
  transfers between devices with their start and end apart: 11, of which 5 were waited for; matrix products, arithmetic and copies ran while one was open for 4% of the time, Pallas kernels for 0%

profile of v1, /device:TPU:0, one launch (start us, length us, event | category | flops | bytes accessed | tf_op | source)
XLA Modules:
  0.0 154.1 jit_solution(2498499326531485947)
XLA Ops:
  1.3 2.0 %request.1 = (s32[24]{0:T(128)}, s32[24]{0:T(128)}) custom-call(s32[1,1,24]{2,1,0:T(1,128)} %lists.1, s32[1,1]{1,0:T(1,128)S(6)} %copy.22.count, s32[3072]{0:T(1024)} %order.1), custom_call_target="tpu_custom_call" | custom-call | tf_op jit(solution)/shard_map/request/pallas_call | solution.py:617
  3.3 1.3 all_to_all.12
  4.7 7.3 %all-to-all-start = ((s32[8,1,3]{2,1,0:T(1,128)}), s32[8,1,3]{2,1,0:T(1,128)S(1)}, u32[]{:S(2)}, u32[]{:S(2)}) async-start(s32[8,1,3]{2,1,0:T(1,128)} %bitcast), calls=%async_computation | async-start | bytes 8192 | tf_op jit(solution)/shard_map/all_to_all | solution.py:625
  11.9 5.2 %copy.19.gaussians = f32[96,59,128]{2,1,0:T(8,128)} copy(f32[96,59,128]{2,0,1:T(8,128)} %param.11) | data formatting | bytes 5799936 | tf_op args[0]
  17.1 1.2 all-to-all-done
  20.2 4.9 %serve.1 = (f32[8,32,128]{2,1,0:T(8,128)}, f32[24,59,128]{2,1,0:T(8,128)}, f32[96,59,128]{2,1,0:T(8,128)}) custom-call(s32[24]{0:T(128)} %reshape.15.asked, f32[96,59,128]{2,1,0:T(8,128)} %copy.19.gaussians), custom_call_target="tpu_custom_call" | custom-call | tf_op jit(solution)/shard_map/serve/pallas_call | solution.py:629
  25.1 4.8 %all-to-all-start.1 = ((f32[8,32,128]{2,1,0:T(8,128)}), f32[8,32,128]{2,1,0:T(8,128)S(1)}, u32[]{:S(2)}, u32[]{:S(2)}) async-start(f32[8,32,128]{2,1,0:T(8,128)} %get-tuple-element.16), calls=%async_computation.1 | async-start | bytes 262144 | tf_op jit(solution)/shard_map/all_to_all | solution.py:642
  30.6 6.7 %all-to-all-done.1.recv = f32[8,32,128]{2,1,0:T(8,128)S(1)} async-done(((f32[8,32,128]{2,1,0:T(8,128)}), f32[8,32,128]{2,1,0:T(8,128)S(1)}, u32[]{:S(2)}, u32[]{:S(2)}) %all-to-all-start.1) | async-done | bytes 131104 | tf_op jit(solution)/shard_map/all_to_all | solution.py:642
  37.9 11.3 %forward.1 = (bf16[3072,128]{1,0:T(8,128)(2,1)}, f32[24,8,1024]{2,1,0:T(8,128)}, f32[8,1024]{1,0:T(8,128)}, f32[3,8,1024]{2,1,0:T(8,128)}, f32[48,128]{1,0:T(8,128)}) custom-call(s32[24]{0:T(128)} %get-tuple-element.15.slot, f32[8,32,128]{2,1,0:T(8,128)} %copy-done.1, bf16[128,1408]{1,0:T(8,128)(2,1)} %constant.15.clone.planes, f32[24,128]{1,0:T(8,128)} %reshape.16.target), custom_call_target="tpu_custom_call" | custom-call | tf_op jit(solution)/shard_map/forward/pallas_call | solution.py:645
  49.2 1.3 collective-permute-start
  50.5 3.8 %collective-permute-start.1 = (f32[48,128]{1,0:T(8,128)}, f32[48,128]{1,0:T(8,128)S(1)}, u32[]{:S(2)}, u32[]{:S(2)}) collective-permute-start(f32[48,128]{1,0:T(8,128)} %get-tuple-element.21.refs_4_), channel_id=1, source_target_pairs={{0,8},{1,9},{2,10},{3,11},{4,12},{5,13},{6,14},{7,15},{8,16},{9,17... | collective-permute-start | bytes 73736 | tf_op jit(solution)/shard_map/ppermute | solution.py:596
  54.9 4.8 %collective-permute-start.3 = (f32[48,128]{1,0:T(8,128)}, f32[48,128]{1,0:T(8,128)S(1)}, u32[]{:S(2)}, u32[]{:S(2)}) collective-permute-start(f32[48,128]{1,0:T(8,128)} %get-tuple-element.21.refs_4_), channel_id=1, source_target_pairs={{0,1},{1,2},{2,3},{3,4},{4,5},{5,6},{6,7},{8,9},{9,10},{10,11},{11... | collective-permute-start | bytes 73736 | tf_op jit(solution)/shard_map/ppermute | solution.py:596
  59.7 1.3 collective-permute-start.4
  61.7 1.3 collective-permute-start.6
  63.1 1.3 collective-permute-start.7
  64.4 1.3 collective-permute-done.4.refs_5_
  65.7 2.9 %collective-permute-done.6.refs_7_ = f32[48,128]{1,0:T(8,128)S(1)} collective-permute-done((f32[48,128]{1,0:T(8,128)}, f32[48,128]{1,0:T(8,128)S(1)}, u32[]{:S(2)}, u32[]{:S(2)}) %collective-permute-start.6) | collective-permute-done | bytes 24608 | tf_op jit(solution)/shard_map/ppermute | solution.py:596
  68.5 5.3 %collective-permute-done.7.refs_8_ = f32[48,128]{1,0:T(8,128)S(1)} collective-permute-done((f32[48,128]{1,0:T(8,128)}, f32[48,128]{1,0:T(8,128)S(1)}, u32[]{:S(2)}, u32[]{:S(2)}) %collective-permute-start.7) | collective-permute-done | bytes 24608 | tf_op jit(solution)/shard_map/ppermute | solution.py:596
  74.5 4.3 %score.1 = (f32[24,128]{1,0:T(8,128)}, f32[1]{0:T(128)}) custom-call(f32[48,128]{1,0:T(8,128)} %copy-done.3, f32[48,128]{1,0:T(8,128)} %copy-done.4, f32[48,128]{1,0:T(8,128)} %copy-done.5, f32[48,128]{1,0:T(8,128)} %copy-done.6, f32[48,128]{1,0:T(8,128)} %get-tuple-element.21.refs_4_, f32[48,128]{1,0:T(8,128)} %copy-done.7, f32[48,128]{1,0:T(8,128)} %copy-done.8, ...), custom_call_target="tpu_custom_call" | custom-call | tf_op jit(solution)/shard_map/score/pallas_call | solution.py:666
  78.8 15.9 %backward.1 = f32[8,32,128]{2,1,0:T(8,128)} custom-call(s32[24]{0:T(128)} %get-tuple-element.15.slot, bf16[3072,128]{1,0:T(8,128)(2,1)} %get-tuple-element.17.table, f32[24,8,1024]{2,1,0:T(8,128)} %get-tuple-element.18.checks, f32[8,1024]{1,0:T(8,128)} %get-tuple-element.19.prefix, f32[3,8,1024]{2,1,0:T(8,128)} %get-tuple-element.20.behind, ...), custom_call_target="tpu_custom_call" | custom-call | tf_op jit(solution)/shard_map/backward/pallas_call | solution.py:675
  94.7 3.4 %all-to-all-start.2 = ((f32[8,32,128]{2,1,0:T(8,128)}), f32[8,32,128]{2,1,0:T(8,128)S(1)}, u32[]{:S(2)}, u32[]{:S(2)}) async-start(f32[8,32,128]{2,1,0:T(8,128)} %backward.1), calls=%async_computation.2 | async-start | bytes 262144 | tf_op jit(solution)/shard_map/all_to_all | solution.py:694
  98.1 43.4 %psum.7 = f32[]{:T(128)} all-reduce(f32[]{:T(128)} %bitcast.1), channel_id=1, replica_groups=mesh['ty'=4,'tx'=8] {'ty','tx'}, use_global_device_ids=true, to_apply=%region_0.0 | all-reduce | flops 1 | bytes 8 | tf_op jit(solution)/shard_map/psum | solution.py:674
  142.8 5.0 %gather.1 = f32[96,59,128]{2,1,0:T(8,128)} custom-call(s32[24]{0:T(128)} %reshape.15.asked, f32[8,32,128]{2,1,0:T(8,128)} %copy-done, f32[24,59,128]{2,1,0:T(8,128)} %get-tuple-element.23.raw, f32[96,59,128]{2,1,0:T(8,128)} %get-tuple-element.24.empty), custom_call_target="tpu_custom_call", output_to_operand_aliasing={{}: (3, {})} | custom-call | tf_op jit(solution)/shard_map/gather/pallas_call | solution.py:695
  147.8 5.2 %copy.20 = f32[96,59,128]{2,0,1:T(8,128)} copy(f32[96,59,128]{2,1,0:T(8,128)} %gather.1) | data formatting | bytes 5799936
  (34 shorter events, 5.8 us)
Async XLA Ops:
  4.7 13.7 %all-to-all-start = ((s32[8,1,3]{2,1,0:T(1,128)}), s32[8,1,3]{2,1,0:T(1,128)S(1)}, u32[]{:S(2)}, u32[]{:S(2)}) async-start(s32[8,1,3]{2,1,0:T(1,128)} %bitcast), calls=%async_computation | async-start | bytes 8192 | tf_op jit(solution)/shard_map/all_to_all | solution.py:625
  17.1 12.8 %copy-start.2 = (f32[3,32,32]{2,1,0:T(8,128)S(1)}, f32[3,32,32]{2,1,0:T(8,128)}, u32[]{:S(2)}) copy-start(f32[3,32,32]{2,1,0:T(8,128)} %param.15) | copy-start | bytes 36868
  25.1 12.1 %all-to-all-start.1 = ((f32[8,32,128]{2,1,0:T(8,128)}), f32[8,32,128]{2,1,0:T(8,128)S(1)}, u32[]{:S(2)}, u32[]{:S(2)}) async-start(f32[8,32,128]{2,1,0:T(8,128)} %get-tuple-element.16), calls=%async_computation.1 | async-start | bytes 262144 | tf_op jit(solution)/shard_map/all_to_all | solution.py:642
  37.2 0.7 copy-start.1
  49.2 11.8 %collective-permute-start = (f32[48,128]{1,0:T(8,128)}, f32[48,128]{1,0:T(8,128)S(1)}, u32[]{:S(2)}, u32[]{:S(2)}) collective-permute-start(f32[48,128]{1,0:T(8,128)} %get-tuple-element.21.refs_4_), channel_id=1, source_target_pairs={{0,9},{1,10},{2,11},{3,12},{4,13},{5,14},{6,15},{8,17},{9,18},{10,... | collective-permute-start | bytes 73736 | tf_op jit(solution)/shard_map/ppermute | solution.py:596
  50.5 11.2 %collective-permute-start.1 = (f32[48,128]{1,0:T(8,128)}, f32[48,128]{1,0:T(8,128)S(1)}, u32[]{:S(2)}, u32[]{:S(2)}) collective-permute-start(f32[48,128]{1,0:T(8,128)} %get-tuple-element.21.refs_4_), channel_id=1, source_target_pairs={{0,8},{1,9},{2,10},{3,11},{4,12},{5,13},{6,14},{7,15},{8,16},{9,17... | collective-permute-start | bytes 73736 | tf_op jit(solution)/shard_map/ppermute | solution.py:596
  54.3 8.8 %collective-permute-start.2 = (f32[48,128]{1,0:T(8,128)}, f32[48,128]{1,0:T(8,128)S(1)}, u32[]{:S(2)}, u32[]{:S(2)}) collective-permute-start(f32[48,128]{1,0:T(8,128)} %get-tuple-element.21.refs_4_), channel_id=1, source_target_pairs={{1,8},{2,9},{3,10},{4,11},{5,12},{6,13},{7,14},{9,16},{10,17},{11,... | collective-permute-start | bytes 73736 | tf_op jit(solution)/shard_map/ppermute | solution.py:596
  54.9 9.4 %collective-permute-start.3 = (f32[48,128]{1,0:T(8,128)}, f32[48,128]{1,0:T(8,128)S(1)}, u32[]{:S(2)}, u32[]{:S(2)}) collective-permute-start(f32[48,128]{1,0:T(8,128)} %get-tuple-element.21.refs_4_), channel_id=1, source_target_pairs={{0,1},{1,2},{2,3},{3,4},{4,5},{5,6},{6,7},{8,9},{9,10},{10,11},{11... | collective-permute-start | bytes 73736 | tf_op jit(solution)/shard_map/ppermute | solution.py:596
  59.7 5.9 %collective-permute-start.4 = (f32[48,128]{1,0:T(8,128)}, f32[48,128]{1,0:T(8,128)S(1)}, u32[]{:S(2)}, u32[]{:S(2)}) collective-permute-start(f32[48,128]{1,0:T(8,128)} %get-tuple-element.21.refs_4_), channel_id=1, source_target_pairs={{1,0},{2,1},{3,2},{4,3},{5,4},{6,5},{7,6},{9,8},{10,9},{11,10},{12... | collective-permute-start | bytes 73736 | tf_op jit(solution)/shard_map/ppermute | solution.py:596
  61.0 12.8 %copy-start.3 = (f32[48,128]{1,0:T(8,128)}, f32[48,128]{1,0:T(8,128)S(1)}, u32[]{:S(2)}) copy-start(f32[48,128]{1,0:T(8,128)S(1)} %collective-permute-done.refs_0_) | copy-start | bytes 73732
  61.1 4.6 %collective-permute-start.5 = (f32[48,128]{1,0:T(8,128)}, f32[48,128]{1,0:T(8,128)S(1)}, u32[]{:S(2)}, u32[]{:S(2)}) collective-permute-start(f32[48,128]{1,0:T(8,128)} %get-tuple-element.21.refs_4_), channel_id=1, source_target_pairs={{8,1},{9,2},{10,3},{11,4},{12,5},{13,6},{14,7},{16,9},{17,10},{18,... | collective-permute-start | bytes 73736 | tf_op jit(solution)/shard_map/ppermute | solution.py:596
  61.7 12.1 %copy-start.4 = (f32[48,128]{1,0:T(8,128)}, f32[48,128]{1,0:T(8,128)S(1)}, u32[]{:S(2)}) copy-start(f32[48,128]{1,0:T(8,128)S(1)} %collective-permute-done.1.refs_1_) | copy-start | bytes 73732
  61.7 6.8 %collective-permute-start.6 = (f32[48,128]{1,0:T(8,128)}, f32[48,128]{1,0:T(8,128)S(1)}, u32[]{:S(2)}, u32[]{:S(2)}) collective-permute-start(f32[48,128]{1,0:T(8,128)} %get-tuple-element.21.refs_4_), channel_id=1, source_target_pairs={{8,0},{9,1},{10,2},{11,3},{12,4},{13,5},{14,6},{15,7},{16,8},{17,9... | collective-permute-start | bytes 73736 | tf_op jit(solution)/shard_map/ppermute | solution.py:596
  63.1 10.8 %copy-start.5 = (f32[48,128]{1,0:T(8,128)}, f32[48,128]{1,0:T(8,128)S(1)}, u32[]{:S(2)}) copy-start(f32[48,128]{1,0:T(8,128)S(1)} %collective-permute-done.2.refs_2_) | copy-start | bytes 73732
  63.1 10.8 %collective-permute-start.7 = (f32[48,128]{1,0:T(8,128)}, f32[48,128]{1,0:T(8,128)S(1)}, u32[]{:S(2)}, u32[]{:S(2)}) collective-permute-start(f32[48,128]{1,0:T(8,128)} %get-tuple-element.21.refs_4_), channel_id=1, source_target_pairs={{9,0},{10,1},{11,2},{12,3},{13,4},{14,5},{15,6},{17,8},{18,9},{19,... | collective-permute-start | bytes 73736 | tf_op jit(solution)/shard_map/ppermute | solution.py:596
  64.4 9.5 %copy-start.6 = (f32[48,128]{1,0:T(8,128)}, f32[48,128]{1,0:T(8,128)S(1)}, u32[]{:S(2)}) copy-start(f32[48,128]{1,0:T(8,128)S(1)} %collective-permute-done.3.refs_3_) | copy-start | bytes 73732
  65.7 8.2 %copy-start.7 = (f32[48,128]{1,0:T(8,128)}, f32[48,128]{1,0:T(8,128)S(1)}, u32[]{:S(2)}) copy-start(f32[48,128]{1,0:T(8,128)S(1)} %collective-permute-done.4.refs_5_) | copy-start | bytes 73732
  65.7 8.2 %copy-start.8 = (f32[48,128]{1,0:T(8,128)}, f32[48,128]{1,0:T(8,128)S(1)}, u32[]{:S(2)}) copy-start(f32[48,128]{1,0:T(8,128)S(1)} %collective-permute-done.5.refs_6_) | copy-start | bytes 73732
  68.5 5.3 %copy-start.9 = (f32[48,128]{1,0:T(8,128)}, f32[48,128]{1,0:T(8,128)S(1)}, u32[]{:S(2)}) copy-start(f32[48,128]{1,0:T(8,128)S(1)} %collective-permute-done.6.refs_7_) | copy-start | bytes 73732
  73.9 0.6 copy-start.10
  94.7 47.4 %all-to-all-start.2 = ((f32[8,32,128]{2,1,0:T(8,128)}), f32[8,32,128]{2,1,0:T(8,128)S(1)}, u32[]{:S(2)}, u32[]{:S(2)}) async-start(f32[8,32,128]{2,1,0:T(8,128)} %backward.1), calls=%async_computation.2 | async-start | bytes 262144 | tf_op jit(solution)/shard_map/all_to_all | solution.py:694
  142.1 0.6 copy-start
